TPU v7x, 32 devices: a whole 2x2x4 slice. The times are simulated.
32 devices in a mesh: parts: 2 (over x), param: 16 (over z, y, core).
Axes of the slice: x: 2, y: 2, z: 4, core: 2. Of those that a mesh axis runs over, the one named last changes fastest.
Arguments:
- inputs: bfloat16 [8192, 4096], P(('parts', 'param')), parts along dimension 0, may hold values from -7 to 7
- out_grads: bfloat16 [8192, 14336], P(('parts', 'param')), parts along dimension 0, may hold values from -7 to 7
- lengths: int32 [32], P(('parts', 'param')), parts along dimension 0, may hold values from 128 to 256, as said below
- example_ids: int32 [32], P(('parts', 'param')), parts along dimension 0, may hold values from 0 to 15, each once
- proj_seeds: int32 [4], P('parts'), parts along dimension 0, may hold values from 1 to 29999
Outputs:
- fisher: float32 [16384, 8192], P(('parts', 'param')), parts along dimension 0
- precond: float32 [32, 8192], P(('parts', 'param')), parts along dimension 0
- kernel: float32 [32, 16], P(('parts', 'param')), parts along dimension 0
There are 2 independent parts, one for each index of `parts`. A program takes and returns all parts, laid end to end along the dimension named above; each array names one. Nothing has to cross between parts.
Inputs may be any that keep to these rules, and one draw needn't show every extreme that they name: `lengths`: each length is a multiple of 128; some example has the full 256 tokens and some has only 128. `example_ids`: a permutation of the group's example indices.
All inputs are finite; a program needn't handle non-finite values.
Results may differ from a plain program's by a relative error of at most 0.007.
The roundings to bfloat16 on the way count: a program that leaves them out, or rounds other values in their place, can miss the bound.
Values may be sent and summed in bfloat16 or wider, within the bound.
A program may use at most 64 MiB of HBM per device.

v0:
```python
import math
import jax
import jax.numpy as jnp
from jax import lax
from jax.sharding import PartitionSpec as P

K_IN = 64
K_OUT = 128
damp_ratio = 0.5


def projection_table(out_dim, fan_in, seed_value):
    row_index = lax.broadcasted_iota(jnp.int32, (fan_in, out_dim), 1)
    col_index = lax.broadcasted_iota(jnp.int32, (fan_in, out_dim), 0)
    hashed = (row_index * 7919 + col_index * 3571 + seed_value * 9973) % 65521
    hashed = hashed * (hashed % 509 + 17) % 65521
    hashed = (hashed * 97 + row_index * 31 + col_index) % 65521
    uniform = hashed.astype(jnp.float32) * (2.0 / 65520.0) - 1.0
    return (uniform * math.sqrt(3.0 / fan_in)).astype(jnp.bfloat16)


def local(inputs, out_grads, lengths, example_ids, proj_seeds):
    highest = lax.Precision.HIGHEST
    ex_dev = lengths.shape[0]
    slot_len = inputs.shape[0] // ex_dev
    table_in = projection_table(K_IN, inputs.shape[1], proj_seeds[0])
    table_out = projection_table(K_OUT, out_grads.shape[1], proj_seeds[1])
    proj_in = jnp.dot(inputs, table_in, preferred_element_type=jnp.float32).astype(jnp.bfloat16)
    proj_out = jnp.dot(out_grads, table_out, preferred_element_type=jnp.float32).astype(
        jnp.bfloat16
    )
    live_rows = (lax.broadcasted_iota(jnp.int32, (ex_dev, slot_len), 1) < lengths[:, None]).reshape(
        ex_dev * slot_len, 1
    )
    proj_in = jnp.where(live_rows, proj_in, jnp.zeros_like(proj_in))
    outer = jnp.einsum(
        "esi,eso->eio",
        proj_in.reshape(ex_dev, slot_len, K_IN),
        proj_out.reshape(ex_dev, slot_len, K_OUT),
        preferred_element_type=jnp.float32,
    )
    gradients = (
        (outer * (1.0 / math.sqrt(slot_len))).reshape(ex_dev, K_IN * K_OUT).astype(jnp.bfloat16)
    )
    gathered, all_ids = (
        lax.all_gather(gradients, "param", axis=0, tiled=True),
        lax.all_gather(example_ids, "param", axis=0, tiled=True),
    )
    example_count = gathered.shape[0]
    proj_width = gathered.shape[1]
    block_rows = proj_width // lax.axis_size("param")
    column_block = lax.dynamic_slice_in_dim(
        gathered, lax.axis_index("param") * block_rows, block_rows, 1
    )
    fisher = (
        lax.dot_general(
            column_block, gathered, (((0,), (0,)), ((), ())), preferred_element_type=jnp.float32
        )
        / example_count
    )
    damping = (
        damp_ratio
        * jnp.sum(jnp.square(gathered.astype(jnp.float32)))
        / (example_count * proj_width)
    )
    gram_matrix = lax.dot_general(
        gathered, gathered, (((1,), (1,)), ((), ())), preferred_element_type=jnp.float32
    )
    system = gram_matrix + damping * example_count * jnp.eye(example_count, dtype=jnp.float32)
    factor = jnp.linalg.cholesky(system)
    solved = jax.scipy.linalg.cho_solve((factor, True), gram_matrix)
    first_slot = lax.axis_index("param") * ex_dev
    own_cols = lax.dynamic_slice_in_dim(solved, first_slot, ex_dev, 1)
    correction = jnp.einsum(
        "jr,jp->rp", own_cols, gathered, precision=highest, preferred_element_type=jnp.float32
    )
    precond = (gradients.astype(jnp.float32) - correction) / damping
    slot_numbers = lax.broadcasted_iota(jnp.int32, (example_count,), 0)
    inverse = jnp.zeros((example_count,), jnp.int32).at[all_ids].set(slot_numbers)
    own_slots = inverse[first_slot + lax.broadcasted_iota(jnp.int32, (ex_dev,), 0)]
    own_grads = jnp.take(gathered, own_slots, axis=0)
    tile_block = lax.dot_general(
        own_grads,
        lax.all_gather(precond.astype(jnp.bfloat16), "param", axis=0, tiled=True),
        (((1,), (1,)), ((), ())),
        preferred_element_type=jnp.float32,
    )
    kernel = (
        jnp.zeros((ex_dev, example_count), jnp.float32).at[:, all_ids].set(tile_block) / proj_width
    )
    return (fisher, precond, kernel)


def solution(mesh):
    placed = (
        P(("parts", "param"), None),
        P(("parts", "param"), None),
        P(("parts", "param")),
        P(("parts", "param")),
        P("parts"),
    )
    return jax.shard_map(
        local,
        mesh=mesh,
        in_specs=placed,
        out_specs=(
            P(("parts", "param"), None),
            P(("parts", "param"), None),
            P(("parts", "param"), None),
        ),
        check_vma=False,
    )
```

profile of v0, /device:TPU:0, one launch (start us, length us, event | category | flops | bytes accessed | tf_op | source)
XLA Modules:
  0.0 117.9 jit_solution(8692307448393772548)
XLA Ops:
  0.6 0.0 copy-start
  2.1 1.2 %dynamic-slice.7 = u32[1]{0:T(128)} dynamic-slice(u32[32]{0:T(128)} %constant.217, u32[]{:T(128)S(6)} %add.156), dynamic_slice_sizes={1} | dynamic-slice | bytes 12
  3.4 0.8 dynamic-update-slice.5
  4.1 13.7 %all-reduce = s32[16]{0:T(128)S(1)} all-reduce(s32[16]{0:T(128)S(1)} %dynamic-update-slice.5), channel_id=1, replica_groups=mesh['parts'=2,'param'=16] {'param'}, use_global_device_ids=true, to_apply=%add | all-reduce | flops 16 | bytes 128
  17.8 0.6 scatter_custom_fusion
  18.5 0.6 dynamic-slice.5
  21.0 1.3 %fusion.127 = (s32[1]{0:T(128)}, s32[1]{0:T(128)}) fusion(s32[2]{0:T(128)} %param.9), kind=kLoop, calls=%fused_computation.144 | loop fusion | bytes 16 | tf_op jit(solution)/shard_map/slice | solution.py:27
  23.7 0.0 copy-done
  23.7 0.0 copy-start.1
  23.7 5.3 %fusion.58 = bf16[64,256]{1,0:T(8,128)(2,1)S(1)} fusion(bf16[256,4096]{1,0:T(8,128)(2,1)S(1)} %copy-done, s32[64]{0:T(128)S(1)} %get-tuple-element.31, s32[]{:T(128)} %bitcast.1, s32[4096]{0:T(1024)S(1)} %iota_multiply_fusion.1, s32[64]{0:T(128)S(1)} %get-tuple-element.32, pred[256]{0:T(512)(128)(4,1)S(1)} %iota_compare_fusion.3), kind=kOutput, calls=%fused_computation.67 | convolution fusion | flops 143687680 | bytes 2147076 | tf_op jit(solution)/shard_map/dot_general | solution.py:28
  29.0 0.0 copy-done.1
  29.1 32.5 %fusion.52.clone.8 = bf16[128,256]{1,0:T(8,128)(2,1)S(1)} fusion(bf16[256,14336]{1,0:T(8,128)(2,1)S(1)} %copy-done.1, s32[128]{0:T(128)S(1)} %get-tuple-element.33, s32[]{:T(128)} %bitcast.2, s32[14336]{0:T(1024)S(1)} %iota_multiply_fusion, s32[128]{0:T(128)S(1)} %get-tuple-element.34), kind=kOutput, calls=%fused_computation.64.clone.clone.clone.clone.clone.clone.clone.1 | convolution fusion | flops 1005617152 | bytes 7463940 | tf_op jit(solution)/shard_map/dot_general | solution.py:29
  61.5 0.1 fusion.62
  61.7 19.4 %all-gather.1 = bf16[16,1,8192]{2,1,0:T(2,128)(2,1)S(1)} all-gather(bf16[1,1,8192]{2,1,0:T(2,128)(2,1)S(1)} %reshape.155), channel_id=1, replica_groups=mesh['parts'=2,'param'=16] {'param'}, dimensions={0}, use_global_device_ids=true | all-gather | bytes 278528 | tf_op jit(solution)/shard_map/all_gather | solution.py:46
  81.1 0.9 multiply_reduce_fusion
  83.3 0.2 fusion.78
  83.5 0.1 copy.12
  83.6 1.5 %cholesky.16 = f32[16,16]{1,0:T(8,128)S(1)} custom-call(f32[16,16]{1,0:T(8,128)S(1)} %fusion.94), custom_call_target="Cholesky" | custom-call | tf_op jit(solution)/shard_map/jit(cholesky)/cholesky | solution.py:70
  85.1 0.6 compare_reduce_fusion
  85.8 0.6 fusion.88
  86.4 1.2 %custom-call.10 = f32[1,16,16]{1,2,0:T(8,128)S(1)} custom-call(f32[1,16,16]{2,1,0:T(8,128)S(1)} %fusion.88), custom_call_target="InvertDiagBlocksLowerTriangular" | custom-call | tf_op jit(solution)/shard_map/jit(_cho_solve)/triangular_solve | solution.py:71
  87.7 0.2 fusion.91
  87.9 0.2 fusion.89
  88.1 0.3 fusion.81
  88.4 0.6 fusion.125
  89.0 19.0 %all-gather = bf16[131072]{0:T(1024)(128)(2,1)S(1)} all-gather(bf16[8192]{0:T(1024)(128)(2,1)S(1)} %get-tuple-element.25), channel_id=2, replica_groups=mesh['parts'=2,'param'=16] {'param'}, dimensions={0}, use_global_device_ids=true | all-gather | bytes 278528 | tf_op jit(solution)/shard_map/all_gather | solution.py:84
  107.9 0.1 reshape.146
  108.1 0.2 convolution_bitcast_fusion
  108.3 0.6 scatter_custom_fusion.1
  108.9 0.5 multiply_bitcast_fusion
  109.4 8.5 %convolution_multiply_fusion = f32[512,8192]{1,0:T(8,128)} fusion(bf16[16,1,8192]{2,0,1:T(8,128)(2,1)S(1)} %get-tuple-element.28, bf16[16,1,512]{2,1,0:T(2,128)(2,1)S(1)} %constant_dynamic-slice_fusion.1), kind=kOutput, calls=%fused_computation.2 | convolution fusion | flops 138412032 | bytes 17055744 | tf_op jit(solution)/shard_map/dot_general | solution.py:56
  (12 shorter events, 0.1 us)
Async XLA Ops:
  0.6 23.0 %copy-start = (bf16[256,4096]{1,0:T(8,128)(2,1)S(1)}, bf16[256,4096]{1,0:T(8,128)(2,1)}, u32[]{:S(2)}) copy-start(bf16[256,4096]{1,0:T(8,128)(2,1)} %param.5) | copy-start | bytes 6291460
  23.7 5.4 %copy-start.1 = (bf16[256,14336]{1,0:T(8,128)(2,1)S(1)}, bf16[256,14336]{1,0:T(8,128)(2,1)}, u32[]{:S(2)}) copy-start(bf16[256,14336]{1,0:T(8,128)(2,1)} %param.6) | copy-start | bytes 22020100
where the time goes:
time: 118 us
  blocking collectives  52.1 us (44%)
  matrix products  47.6 us (40%)
  between operations  6.76 us (6%)
  other arithmetic  6.11 us (5%)
  local copies, waits for them, and re-layouts  5.43 us (5%)
    dot_general x1, matrix products, local(): jnp.dot(out_grads, table_out, preferred_element_type=jnp.float32)  32.5 us
    all_gather x1, blocking collectives, local(): lax.all_gather(gradients, 'param', axis=0, tiled=True)  19.4 us
    all_gather x1, blocking collectives, local(): lax.all_gather(precond.astype(jnp.bfloat16), 'param', axis=0, tiled=True)  19 us
    unnamed x1, blocking collectives  13.7 us
    dot_general x1, matrix products, local(): lax.dot_general(column_block, gathered, (((0,), (0,)), ((), ())), preferr...  8.53 us
    dot_general x1, matrix products, local(): jnp.dot(inputs, table_in, preferred_element_type=jnp.float32)  5.35 us

commit v1 on v0

--- a/solution.py
+++ b/solution.py
@@ -7,6 +7,27 @@
 K_IN = 64
 K_OUT = 128
 damp_ratio = 0.5
+
+
+def ring_gather(x, axis, dim):
+    count, mine, span = (lax.axis_size(axis), lax.axis_index(axis), x.shape[dim])
+    right = [(i, (i + 1) % count) for i in range(count)]
+    behind = [(i, (i - 1) % count) for i in range(count)]
+    filled = jnp.zeros((*x.shape[:dim], count * span, *x.shape[dim + 1 :]), x.dtype)
+    filled = lax.dynamic_update_slice_in_dim(filled, x, mine * span, axis=dim)
+    from_left = from_right = x
+    halfway = count // 2
+    for step in range(1, halfway + 1):
+        from_left = lax.ppermute(from_left, axis, right)
+        filled = lax.dynamic_update_slice_in_dim(
+            filled, from_left, (mine - step) % count * span, axis=dim
+        )
+        if step < count - halfway:
+            from_right = lax.ppermute(from_right, axis, behind)
+            filled = lax.dynamic_update_slice_in_dim(
+                filled, from_right, (mine + step) % count * span, axis=dim
+            )
+    return filled
 
 
 def projection_table(out_dim, fan_in, seed_value):
@@ -81,7 +102,7 @@
     own_grads = jnp.take(gathered, own_slots, axis=0)
     tile_block = lax.dot_general(
         own_grads,
-        lax.all_gather(precond.astype(jnp.bfloat16), "param", axis=0, tiled=True),
+        ring_gather(precond.astype(jnp.bfloat16), "param", 0),
         (((1,), (1,)), ((), ())),
         preferred_element_type=jnp.float32,
     )

time: 118 us -> 141 us (1.19)
  starting transfers between devices: 0 us -> 27.2 us
  blocking collectives: 52.1 us -> 36.6 us
  waiting for transfers between devices: 0 us -> 7.98 us
  local copies, waits for them, and re-layouts: 5.43 us -> 12.4 us
  matrix products: 47.6 us -> 43.1 us
    ppermute x0 -> x15, starting transfers between devices: none -> 27.2 us  [the longest x7 26.3 us: ring_gather(): from_right = lax.ppermute(from_right, axis, behind)]
    all_gather x1 -> x0, blocking collectives: 19 us -> none  [local(): lax.all_gather(precond.astype(jnp.bfloat16), 'param', axis=0, tiled=True)]
    ppermute x0 -> x15, waiting for transfers between devices: none -> 7.98 us  [the longest x8 7.96 us: ring_gather(): from_left = lax.ppermute(from_left, axis, right)]
    dynamic_update_slice x0 -> x16, local copies, waits for them, and re-layouts: none -> 7.6 us  [the longest x8 3.8 us: ring_gather(): lax.dynamic_update_slice_in_dim(filled, from_left, (mine - step) % count...]
    all_gather x1, blocking collectives: 19.4 us -> 24.6 us  [local(): lax.all_gather(gradients, 'param', axis=0, tiled=True)]
    dot_general x1, matrix products: 32.5 us -> 28 us  [local(): jnp.dot(out_grads, table_out, preferred_element_type=jnp.float32)]
    unnamed x1, blocking collectives: 13.7 us -> 12.1 us
  transfers between devices with their start and end apart: 0 -> 15, of which waited for: 0 -> 5; matrix products, arithmetic and copies ran while one was open for 0% -> 13% of each run, Pallas kernels for 0% -> 0%
where the time goes in v1:
time: 141 us
  matrix products  43.1 us (31%)
  blocking collectives  36.6 us (26%)
  starting transfers between devices  27.2 us (19%)
  local copies, waits for them, and re-layouts  12.4 us (9%)
  waiting for transfers between devices  7.98 us (6%)
  between operations  7.18 us (5%)
  other arithmetic  6.1 us (4%)
    dot_general x1, matrix products, local(): jnp.dot(out_grads, table_out, preferred_element_type=jnp.float32)  28 us
    ppermute x7, starting transfers between devices, ring_gather(): from_right = lax.ppermute(from_right, axis, behind)  26.3 us
    all_gather x1, blocking collectives, local(): lax.all_gather(gradients, 'param', axis=0, tiled=True)  24.6 us
    unnamed x1, blocking collectives  12.1 us
    dot_general x1, matrix products, local(): lax.dot_general(column_block, gathered, (((0,), (0,)), ((), ())), preferr...  8.53 us
    ppermute x8, waiting for transfers between devices, ring_gather(): from_left = lax.ppermute(from_left, axis, right)  7.96 us
    dot_general x1, matrix products, local(): jnp.dot(inputs, table_in, preferred_element_type=jnp.float32)  5.35 us
    dynamic_update_slice x8, local copies, waits for them, and re-layouts, ring_gather(): lax.dynamic_update_slice_in_dim(filled, from_left, (mine - step) % count...  3.8 us
  transfers between devices with their start and end apart: 15, of which 5 were waited for; matrix products, arithmetic and copies ran while one was open for 13% of the time, Pallas kernels for 0%

profile of v1, /device:TPU:0, one launch (start us, length us, event | category | flops | bytes accessed | tf_op | source)
XLA Modules:
  0.0 140.6 jit_solution(5934825366307074963)
XLA Ops:
  0.6 0.0 copy-start
  1.5 1.3 fusion.127
  4.1 28.0 %fusion.52.clone.8 = bf16[128,256]{1,0:T(8,128)(2,1)S(1)} fusion(bf16[256,14336]{1,0:T(8,128)(2,1)} %param.6, s32[128]{0:T(128)S(1)} %get-tuple-element.33, s32[]{:T(128)} %bitcast.2, s32[14336]{0:T(1024)S(1)} %iota_multiply_fusion, s32[128]{0:T(128)S(1)} %get-tuple-element.34), kind=kOutput, calls=%fused_computation.64.clone.clone.clone.clone.clone.clone.clone.1 | convolution fusion | flops 1005617152 | bytes 7463940 | tf_op jit(solution)/shard_map/dot_general | solution.py:50
  32.2 5.3 %fusion.58 = bf16[64,256]{1,0:T(8,128)(2,1)S(1)} fusion(bf16[256,4096]{1,0:T(8,128)(2,1)S(1)} %copy-done, s32[64]{0:T(128)S(1)} %get-tuple-element.31, s32[]{:T(128)} %bitcast.1, s32[4096]{0:T(1024)S(1)} %iota_multiply_fusion.1, s32[64]{0:T(128)S(1)} %get-tuple-element.32, pred[256]{0:T(512)(128)(4,1)S(1)} %iota_compare_fusion.3), kind=kOutput, calls=%fused_computation.67 | convolution fusion | flops 143687680 | bytes 2147076 | tf_op jit(solution)/shard_map/dot_general | solution.py:49
  37.5 0.0 copy-start.1
  37.5 0.1 fusion.62
  37.7 24.6 %all-gather = bf16[16,1,8192]{2,1,0:T(2,128)(2,1)S(1)} all-gather(bf16[1,1,8192]{2,1,0:T(2,128)(2,1)S(1)} %reshape.154), channel_id=1, replica_groups=mesh['parts'=2,'param'=16] {'param'}, dimensions={0}, use_global_device_ids=true | all-gather | bytes 278528 | tf_op jit(solution)/shard_map/all_gather | solution.py:67
  62.3 0.9 multiply_reduce_fusion
  64.5 0.2 fusion.78
  64.7 0.1 copy.12
  64.7 1.5 %cholesky.16 = f32[16,16]{1,0:T(8,128)S(1)} custom-call(f32[16,16]{1,0:T(8,128)S(1)} %fusion.94), custom_call_target="Cholesky" | custom-call | tf_op jit(solution)/shard_map/jit(cholesky)/cholesky | solution.py:91
  66.3 0.6 compare_reduce_fusion
  66.9 0.6 fusion.88
  67.6 1.2 custom-call.10
  68.8 0.2 fusion.91
  69.0 0.2 fusion.89
  69.2 0.3 fusion.81
  69.5 0.6 fusion.125
  70.1 0.4 collective-permute-start
  70.5 4.1 %collective-permute-start.1 = (bf16[1,8192]{1,0:T(2,128)(2,1)S(1)}, bf16[1,8192]{1,0:T(2,128)(2,1)S(1)}, u32[]{:S(2)}, u32[]{:S(2)}) collective-permute-start(bf16[1,8192]{1,0:T(2,128)(2,1)S(1)} %convert_element_type.64), channel_id=1, source_target_pairs={{0,15},{1,0},{2,1},{3,2},{4,3},{5,4},{6,5},{7,6},{8,7},{9,8},{10,9... | collective-permute-start | bytes 49160 | tf_op jit(solution)/shard_map/ppermute | solution.py:26
  74.6 1.6 %collective-permute-done = bf16[1,8192]{1,0:T(2,128)(2,1)S(1)} collective-permute-done((bf16[1,8192]{1,0:T(2,128)(2,1)S(1)}, bf16[1,8192]{1,0:T(2,128)(2,1)S(1)}, u32[]{:S(2)}, u32[]{:S(2)}) %collective-permute-start) | collective-permute-done | bytes 16416 | tf_op jit(solution)/shard_map/ppermute | solution.py:21
  76.2 4.4 %collective-permute-start.3 = (bf16[1,8192]{1,0:T(2,128)(2,1)S(1)}, bf16[1,8192]{1,0:T(2,128)(2,1)S(1)}, u32[]{:S(2)}, u32[]{:S(2)}) collective-permute-start(bf16[1,8192]{1,0:T(2,128)(2,1)S(1)} %collective-permute-done.1), channel_id=1, source_target_pairs={{0,15},{1,0},{2,1},{3,2},{4,3},{5,4},{6,5},{7,6},{8,7},{9,8},{10,9... | collective-permute-start | bytes 49160 | tf_op jit(solution)/shard_map/ppermute | solution.py:26
  80.7 1.6 %collective-permute-done.2 = bf16[1,8192]{1,0:T(2,128)(2,1)S(1)} collective-permute-done((bf16[1,8192]{1,0:T(2,128)(2,1)S(1)}, bf16[1,8192]{1,0:T(2,128)(2,1)S(1)}, u32[]{:S(2)}, u32[]{:S(2)}) %collective-permute-start.2) | collective-permute-done | bytes 16416 | tf_op jit(solution)/shard_map/ppermute | solution.py:21
  82.3 0.0 collective-permute-start.4
  82.3 0.0 collective-permute-done.3
  82.3 4.4 %collective-permute-start.5 = (bf16[1,8192]{1,0:T(2,128)(2,1)S(1)}, bf16[1,8192]{1,0:T(2,128)(2,1)S(1)}, u32[]{:S(2)}, u32[]{:S(2)}) collective-permute-start(bf16[1,8192]{1,0:T(2,128)(2,1)S(1)} %collective-permute-done.3), channel_id=1, source_target_pairs={{0,15},{1,0},{2,1},{3,2},{4,3},{5,4},{6,5},{7,6},{8,7},{9,8},{10,9... | collective-permute-start | bytes 49160 | tf_op jit(solution)/shard_map/ppermute | solution.py:26
  86.7 1.6 %collective-permute-done.4 = bf16[1,8192]{1,0:T(2,128)(2,1)S(1)} collective-permute-done((bf16[1,8192]{1,0:T(2,128)(2,1)S(1)}, bf16[1,8192]{1,0:T(2,128)(2,1)S(1)}, u32[]{:S(2)}, u32[]{:S(2)}) %collective-permute-start.4) | collective-permute-done | bytes 16416 | tf_op jit(solution)/shard_map/ppermute | solution.py:21
  88.3 0.0 collective-permute-done.5
  88.3 4.4 %collective-permute-start.7 = (bf16[1,8192]{1,0:T(2,128)(2,1)S(1)}, bf16[1,8192]{1,0:T(2,128)(2,1)S(1)}, u32[]{:S(2)}, u32[]{:S(2)}) collective-permute-start(bf16[1,8192]{1,0:T(2,128)(2,1)S(1)} %collective-permute-done.5), channel_id=1, source_target_pairs={{0,15},{1,0},{2,1},{3,2},{4,3},{5,4},{6,5},{7,6},{8,7},{9,8},{10,9... | collective-permute-start | bytes 49160 | tf_op jit(solution)/shard_map/ppermute | solution.py:26
  92.7 1.6 %collective-permute-done.6 = bf16[1,8192]{1,0:T(2,128)(2,1)S(1)} collective-permute-done((bf16[1,8192]{1,0:T(2,128)(2,1)S(1)}, bf16[1,8192]{1,0:T(2,128)(2,1)S(1)}, u32[]{:S(2)}, u32[]{:S(2)}) %collective-permute-start.6) | collective-permute-done | bytes 16416 | tf_op jit(solution)/shard_map/ppermute | solution.py:21
  94.3 0.0 collective-permute-start.8
  94.3 0.0 collective-permute-done.7
  94.3 4.4 %collective-permute-start.9 = (bf16[1,8192]{1,0:T(2,128)(2,1)S(1)}, bf16[1,8192]{1,0:T(2,128)(2,1)S(1)}, u32[]{:S(2)}, u32[]{:S(2)}) collective-permute-start(bf16[1,8192]{1,0:T(2,128)(2,1)S(1)} %collective-permute-done.7), channel_id=1, source_target_pairs={{0,15},{1,0},{2,1},{3,2},{4,3},{5,4},{6,5},{7,6},{8,7},{9,8},{10,9... | collective-permute-start | bytes 49160 | tf_op jit(solution)/shard_map/ppermute | solution.py:26
  98.8 1.6 %collective-permute-done.8 = bf16[1,8192]{1,0:T(2,128)(2,1)S(1)} collective-permute-done((bf16[1,8192]{1,0:T(2,128)(2,1)S(1)}, bf16[1,8192]{1,0:T(2,128)(2,1)S(1)}, u32[]{:S(2)}, u32[]{:S(2)}) %collective-permute-start.8) | collective-permute-done | bytes 16416 | tf_op jit(solution)/shard_map/ppermute | solution.py:21
  100.4 0.0 collective-permute-start.10
  101.1 0.6 dynamic-slice.7
  101.7 0.8 dynamic-update-slice.5
  102.4 0.0 collective-permute-done.9
  102.4 4.5 %collective-permute-start.11 = (bf16[1,8192]{1,0:T(2,128)(2,1)S(1)}, bf16[1,8192]{1,0:T(2,128)(2,1)S(1)}, u32[]{:S(2)}, u32[]{:S(2)}) collective-permute-start(bf16[1,8192]{1,0:T(2,128)(2,1)S(1)} %collective-permute-done.9), channel_id=1, source_target_pairs={{0,15},{1,0},{2,1},{3,2},{4,3},{5,4},{6,5},{7,6},{8,7},{9,8},{10,9... | collective-permute-start | bytes 49160 | tf_op jit(solution)/shard_map/ppermute | solution.py:26
  106.9 0.0 collective-permute-done.10
  106.9 8.5 %convolution_multiply_fusion = f32[512,8192]{1,0:T(8,128)} fusion(bf16[16,1,8192]{2,0,1:T(8,128)(2,1)S(1)} %get-tuple-element.28, bf16[16,1,512]{2,1,0:T(2,128)(2,1)S(1)} %constant_dynamic-slice_fusion.1), kind=kOutput, calls=%fused_computation.2 | convolution fusion | flops 138412032 | bytes 17055744 | tf_op jit(solution)/shard_map/dot_general | solution.py:77
  115.4 12.1 %all-reduce = s32[16]{0:T(128)S(1)} all-reduce(s32[16]{0:T(128)S(1)} %dynamic-update-slice.5), channel_id=1, replica_groups=mesh['parts'=2,'param'=16] {'param'}, use_global_device_ids=true, to_apply=%add | all-reduce | flops 16 | bytes 128
  127.5 0.5 collective-permute-start.14
  128.0 0.6 scatter_custom_fusion
  128.7 0.7 dynamic-slice.5
  131.4 0.5 dynamic_update_slice.48
  132.0 0.5 dynamic_update_slice.49
  132.5 0.5 dynamic_update_slice.50
  133.0 0.5 dynamic_update_slice.51
  133.5 0.5 dynamic_update_slice.52
  133.9 0.5 dynamic_update_slice.53
  134.4 0.5 dynamic_update_slice.54
  134.9 0.5 dynamic_update_slice.55
  135.4 0.5 dynamic_update_slice.56
  135.9 0.5 dynamic_update_slice.57
  136.4 0.5 dynamic_update_slice.58
  136.8 0.5 dynamic_update_slice.59
  137.3 0.5 dynamic_update_slice.60
  137.8 0.5 dynamic_update_slice.61
  138.3 0.5 dynamic_update_slice.62
  138.8 0.5 dynamic_update_slice.63
  139.3 0.2 convolution_bitcast_fusion
  139.5 0.6 scatter_custom_fusion.1
  140.1 0.5 multiply_bitcast_fusion
  (25 shorter events, 0.2 us)
Async XLA Ops:
  0.6 31.5 %copy-start = (bf16[256,4096]{1,0:T(8,128)(2,1)S(1)}, bf16[256,4096]{1,0:T(8,128)(2,1)}, u32[]{:S(2)}) copy-start(bf16[256,4096]{1,0:T(8,128)(2,1)} %param.5) | copy-start | bytes 6291460
  37.5 63.6 %copy-start.1 = (u32[32]{0:T(128)S(1)}, u32[32]{0:T(128)}, u32[]{:S(2)}) copy-start(u32[32]{0:T(128)} %constant.315) | copy-start | bytes 388
  70.1 6.1 %collective-permute-start = (bf16[1,8192]{1,0:T(2,128)(2,1)S(1)}, bf16[1,8192]{1,0:T(2,128)(2,1)S(1)}, u32[]{:S(2)}, u32[]{:S(2)}) collective-permute-start(bf16[1,8192]{1,0:T(2,128)(2,1)S(1)} %convert_element_type.64), channel_id=1, source_target_pairs={{0,1},{1,2},{2,3},{3,4},{4,5},{5,6},{6,7},{7,8},{8,9},{9,10},{10,1... | collective-permute-start | bytes 49160 | tf_op jit(solution)/shard_map/ppermute | solution.py:21
  70.5 5.7 %collective-permute-start.1 = (bf16[1,8192]{1,0:T(2,128)(2,1)S(1)}, bf16[1,8192]{1,0:T(2,128)(2,1)S(1)}, u32[]{:S(2)}, u32[]{:S(2)}) collective-permute-start(bf16[1,8192]{1,0:T(2,128)(2,1)S(1)} %convert_element_type.64), channel_id=1, source_target_pairs={{0,15},{1,0},{2,1},{3,2},{4,3},{5,4},{6,5},{7,6},{8,7},{9,8},{10,9... | collective-permute-start | bytes 49160 | tf_op jit(solution)/shard_map/ppermute | solution.py:26
  76.2 6.0 %collective-permute-start.2 = (bf16[1,8192]{1,0:T(2,128)(2,1)S(1)}, bf16[1,8192]{1,0:T(2,128)(2,1)S(1)}, u32[]{:S(2)}, u32[]{:S(2)}) collective-permute-start(bf16[1,8192]{1,0:T(2,128)(2,1)S(1)} %collective-permute-done), channel_id=1, source_target_pairs={{0,1},{1,2},{2,3},{3,4},{4,5},{5,6},{6,7},{7,8},{8,9},{9,10},{10,1... | collective-permute-start | bytes 49160 | tf_op jit(solution)/shard_map/ppermute | solution.py:21
  76.2 6.0 %collective-permute-start.3 = (bf16[1,8192]{1,0:T(2,128)(2,1)S(1)}, bf16[1,8192]{1,0:T(2,128)(2,1)S(1)}, u32[]{:S(2)}, u32[]{:S(2)}) collective-permute-start(bf16[1,8192]{1,0:T(2,128)(2,1)S(1)} %collective-permute-done.1), channel_id=1, source_target_pairs={{0,15},{1,0},{2,1},{3,2},{4,3},{5,4},{6,5},{7,6},{8,7},{9,8},{10,9... | collective-permute-start | bytes 49160 | tf_op jit(solution)/shard_map/ppermute | solution.py:26
  82.3 6.0 %collective-permute-start.4 = (bf16[1,8192]{1,0:T(2,128)(2,1)S(1)}, bf16[1,8192]{1,0:T(2,128)(2,1)S(1)}, u32[]{:S(2)}, u32[]{:S(2)}) collective-permute-start(bf16[1,8192]{1,0:T(2,128)(2,1)S(1)} %collective-permute-done.2), channel_id=1, source_target_pairs={{0,1},{1,2},{2,3},{3,4},{4,5},{5,6},{6,7},{7,8},{8,9},{9,10},{10,1... | collective-permute-start | bytes 49160 | tf_op jit(solution)/shard_map/ppermute | solution.py:21
  82.3 6.0 %collective-permute-start.5 = (bf16[1,8192]{1,0:T(2,128)(2,1)S(1)}, bf16[1,8192]{1,0:T(2,128)(2,1)S(1)}, u32[]{:S(2)}, u32[]{:S(2)}) collective-permute-start(bf16[1,8192]{1,0:T(2,128)(2,1)S(1)} %collective-permute-done.3), channel_id=1, source_target_pairs={{0,15},{1,0},{2,1},{3,2},{4,3},{5,4},{6,5},{7,6},{8,7},{9,8},{10,9... | collective-permute-start | bytes 49160 | tf_op jit(solution)/shard_map/ppermute | solution.py:26
  88.3 6.0 %collective-permute-start.6 = (bf16[1,8192]{1,0:T(2,128)(2,1)S(1)}, bf16[1,8192]{1,0:T(2,128)(2,1)S(1)}, u32[]{:S(2)}, u32[]{:S(2)}) collective-permute-start(bf16[1,8192]{1,0:T(2,128)(2,1)S(1)} %collective-permute-done.4), channel_id=1, source_target_pairs={{0,1},{1,2},{2,3},{3,4},{4,5},{5,6},{6,7},{7,8},{8,9},{9,10},{10,1... | collective-permute-start | bytes 49160 | tf_op jit(solution)/shard_map/ppermute | solution.py:21
  88.3 6.0 %collective-permute-start.7 = (bf16[1,8192]{1,0:T(2,128)(2,1)S(1)}, bf16[1,8192]{1,0:T(2,128)(2,1)S(1)}, u32[]{:S(2)}, u32[]{:S(2)}) collective-permute-start(bf16[1,8192]{1,0:T(2,128)(2,1)S(1)} %collective-permute-done.5), channel_id=1, source_target_pairs={{0,15},{1,0},{2,1},{3,2},{4,3},{5,4},{6,5},{7,6},{8,7},{9,8},{10,9... | collective-permute-start | bytes 49160 | tf_op jit(solution)/shard_map/ppermute | solution.py:26
  94.3 6.0 %collective-permute-start.8 = (bf16[1,8192]{1,0:T(2,128)(2,1)S(1)}, bf16[1,8192]{1,0:T(2,128)(2,1)S(1)}, u32[]{:S(2)}, u32[]{:S(2)}) collective-permute-start(bf16[1,8192]{1,0:T(2,128)(2,1)S(1)} %collective-permute-done.6), channel_id=1, source_target_pairs={{0,1},{1,2},{2,3},{3,4},{4,5},{5,6},{6,7},{7,8},{8,9},{9,10},{10,1... | collective-permute-start | bytes 49160 | tf_op jit(solution)/shard_map/ppermute | solution.py:21
  94.3 8.1 %collective-permute-start.9 = (bf16[1,8192]{1,0:T(2,128)(2,1)S(1)}, bf16[1,8192]{1,0:T(2,128)(2,1)S(1)}, u32[]{:S(2)}, u32[]{:S(2)}) collective-permute-start(bf16[1,8192]{1,0:T(2,128)(2,1)S(1)} %collective-permute-done.7), channel_id=1, source_target_pairs={{0,15},{1,0},{2,1},{3,2},{4,3},{5,4},{6,5},{7,6},{8,7},{9,8},{10,9... | collective-permute-start | bytes 49160 | tf_op jit(solution)/shard_map/ppermute | solution.py:26
  100.4 6.5 %collective-permute-start.10 = (bf16[1,8192]{1,0:T(2,128)(2,1)S(1)}, bf16[1,8192]{1,0:T(2,128)(2,1)S(1)}, u32[]{:S(2)}, u32[]{:S(2)}) collective-permute-start(bf16[1,8192]{1,0:T(2,128)(2,1)S(1)} %collective-permute-done.8), channel_id=1, source_target_pairs={{0,1},{1,2},{2,3},{3,4},{4,5},{5,6},{6,7},{7,8},{8,9},{9,10},{10,1... | collective-permute-start | bytes 49160 | tf_op jit(solution)/shard_map/ppermute | solution.py:21
  102.4 25.1 %collective-permute-start.11 = (bf16[1,8192]{1,0:T(2,128)(2,1)S(1)}, bf16[1,8192]{1,0:T(2,128)(2,1)S(1)}, u32[]{:S(2)}, u32[]{:S(2)}) collective-permute-start(bf16[1,8192]{1,0:T(2,128)(2,1)S(1)} %collective-permute-done.9), channel_id=1, source_target_pairs={{0,15},{1,0},{2,1},{3,2},{4,3},{5,4},{6,5},{7,6},{8,7},{9,8},{10,9... | collective-permute-start | bytes 49160 | tf_op jit(solution)/shard_map/ppermute | solution.py:26
  106.9 20.6 %collective-permute-start.12 = (bf16[1,8192]{1,0:T(2,128)(2,1)S(1)}, bf16[1,8192]{1,0:T(2,128)(2,1)S(1)}, u32[]{:S(2)}, u32[]{:S(2)}) collective-permute-start(bf16[1,8192]{1,0:T(2,128)(2,1)S(1)} %collective-permute-done.10), channel_id=1, source_target_pairs={{0,1},{1,2},{2,3},{3,4},{4,5},{5,6},{6,7},{7,8},{8,9},{9,10},{10,1... | collective-permute-start | bytes 49160 | tf_op jit(solution)/shard_map/ppermute | solution.py:21
  127.5 10.8 %collective-permute-start.13 = (bf16[1,8192]{1,0:T(2,128)(2,1)S(1)}, bf16[1,8192]{1,0:T(2,128)(2,1)S(1)}, u32[]{:S(2)}, u32[]{:S(2)}) collective-permute-start(bf16[1,8192]{1,0:T(2,128)(2,1)S(1)} %collective-permute-done.11), channel_id=1, source_target_pairs={{0,15},{1,0},{2,1},{3,2},{4,3},{5,4},{6,5},{7,6},{8,7},{9,8},{10,9... | collective-permute-start | bytes 49160 | tf_op jit(solution)/shard_map/ppermute | solution.py:26
  127.5 11.3 %collective-permute-start.14 = (bf16[1,8192]{1,0:T(2,128)(2,1)S(1)}, bf16[1,8192]{1,0:T(2,128)(2,1)S(1)}, u32[]{:S(2)}, u32[]{:S(2)}) collective-permute-start(bf16[1,8192]{1,0:T(2,128)(2,1)S(1)} %collective-permute-done.12), channel_id=1, source_target_pairs={{0,1},{1,2},{2,3},{3,4},{4,5},{5,6},{6,7},{7,8},{8,9},{9,10},{10,1... | collective-permute-start | bytes 49160 | tf_op jit(solution)/shard_map/ppermute | solution.py:21
